TPU v7x, 32 devices: a whole 2x2x4 slice. The times are simulated.
32 devices in a mesh: row: 16 (over z, x, core), col: 2 (over y).
Axes of the slice: x: 2, y: 2, z: 4, core: 2. Of those that a mesh axis runs over, the one named last changes fastest.
Arguments:
- dist_first: bfloat16 [32768, 32768], P('row', 'col'), may hold values from -0.34 to 0.34
- coupling: bfloat16 [32768, 256], P('row', 'col'), may hold values from 0.099609375 to 1
- dist_second: bfloat16 [256, 512], P(None, 'col'), may hold values from -12 to 12
- row_potential: float32 [32768], P('row'), may hold values from -150 to 120
- column_cost: float32 [512], P('col'), may hold values from -300 to 20
- column_mass: float32 [512], P('col'), may hold values from 0.5 to 2
Outputs:
- transport: bfloat16 [32768, 512], P('row', 'col')
- potential: float32 [512], P('col')
All inputs are finite; a program needn't handle non-finite values.
Results may differ from a plain program's by a relative error of at most 0.0051.
Values may be sent and summed in bfloat16 or wider, within the bound.
A program may use at most 128 MiB of HBM per device.

v0:
```python
import jax
import jax.numpy as jnp
from jax import lax
from jax.sharding import PartitionSpec as P

N = 32768


def body(dist_first, coupling, dist_second, row_potential, column_cost, column_mass):
    groups = lax.axis_size("col")
    stacked = lax.all_gather(coupling, "row", axis=0, tiled=True)
    total_rows = stacked.shape[0]
    stacked = stacked.reshape(groups, 1, total_rows // groups, stacked.shape[1])
    traded = lax.all_to_all(stacked, "col", split_axis=0, concat_axis=1, tiled=True)
    second_full = lax.all_gather(dist_second, "col", axis=1, tiled=True)
    second_blocks = second_full.reshape(
        groups, second_full.shape[0] // groups, second_full.shape[1]
    )
    product = jnp.einsum(
        "jnk,jkq->nq", traded[0], second_blocks, preferred_element_type=jnp.float32
    ).astype(jnp.bfloat16)
    partial_value = jnp.dot(dist_first, product, preferred_element_type=jnp.float32)
    gradient = lax.psum_scatter(partial_value, "col", scatter_dimension=1, tiled=True)
    scores = row_potential[:, None] + 2.0 * gradient - column_cost[None, :]
    local_high = jnp.max(scores, axis=0)
    highest = lax.pmax(local_high, "row")
    weights = jnp.exp(scores - highest[None, :])
    column_sum = lax.psum(jnp.sum(weights, axis=0), "row")
    potential = jnp.log(column_mass) - highest - jnp.log(column_sum)
    transport = (weights * (N * column_mass / column_sum)[None, :]).astype(jnp.bfloat16)
    return (transport, potential)


def solution(mesh):
    in_specs = (P("row", "col"), P("row", "col"), P(None, "col"), P("row"), P("col"), P("col"))
    out_specs = (P("row", "col"), P("col"))
    return jax.shard_map(body, mesh=mesh, in_specs=in_specs, out_specs=out_specs, check_vma=False)
```

profile of v0, /device:TPU:0, one launch (start us, length us, event | category | flops | bytes accessed | tf_op | source)
XLA Modules:
  0.0 373.1 jit_solution(14393238929022774221)
XLA Ops:
  7.2 0.0 all-gather.2.cloned.1.call-start
  7.2 0.7 all-gather.2.cloned.1.call-update
  7.9 79.9 %all-gather.2.cloned.1.call-done = bf16[32768,128]{1,0:T(8,128)(2,1)} async-done(((bf16[2048,128]{1,0:T(8,128)(2,1)}), bf16[32768,128]{1,0:T(8,128)(2,1)}) %all-gather.2.cloned.1.call-update) | async-done | bytes 8388624 | tf_op jit(solution)/shard_map/all_gather | solution.py:11
  87.8 0.0 copy-start.1
  87.8 7.1 %all-to-all-start = ((bf16[2,1,16384,128]{3,2,1,0:T(8,128)(2,1)}), bf16[2,1,16384,128]{3,2,1,0:T(8,128)(2,1)}, u32[]{:S(2)}, u32[]{:S(2)}) async-start(bf16[2,1,16384,128]{3,2,1,0:T(8,128)(2,1)} %bitcast.31), calls=%async_computation | async-start | bytes 16777216 | tf_op jit(solution)/shard_map/all_to_all | solution.py:14
  94.8 0.0 reduce-scatter.2.cloned.1.call-start
  94.9 0.0 copy-done.1
  94.9 95.7 %all_gather.7 = bf16[256,512]{1,0:T(8,128)(2,1)S(1)} all-gather(bf16[256,256]{1,0:T(8,128)(2,1)S(1)} %copy-done.1), channel_id=1, replica_groups=mesh['row'=16,'col'=2] {'col'}, dimensions={1}, use_global_device_ids=true | all-gather | bytes 393216 | tf_op jit(solution)/shard_map/all_gather | solution.py:15
  190.6 0.0 all-to-all-done
  190.6 11.6 %bitcast_convert_fusion.clone.6 = bf16[16384,512]{1,0:T(8,128)(2,1)} fusion(bf16[2,128,512]{2,1,0:T(8,128)(2,1)S(1)} %bitcast.32, bf16[2,1,16384,128]{3,2,1,0:T(8,128)(2,1)} %all-to-all-done), kind=kOutput, calls=%fused_computation.clone.clone.clone.clone.clone.1 | convolution fusion | flops 4303355904 | bytes 25427968 | tf_op jit(solution)/shard_map/jnk,jkq->nq/dot_general | solution.py:19
  202.2 44.3 %fusion.4 = f32[2048,512]{0,1:T(8,128)} fusion(bf16[2048,16384]{1,0:T(8,128)(2,1)} %param.6, bf16[16384,512]{1,0:T(8,128)(2,1)} %bitcast_convert_fusion.clone.6), kind=kOutput, calls=%fused_computation.3 | convolution fusion | flops 34359738368 | bytes 88080384 | tf_op jit(solution)/shard_map/dot_general | solution.py:22
  246.5 0.0 copy-start.2
  246.5 0.0 copy-start.3
  246.5 0.0 reduce-scatter.2.cloned.1.call-update
  246.5 0.0 copy-start.4
  246.5 51.8 %reduce-scatter.2.cloned.1.call-done = f32[2048,256]{0,1:T(8,128)} async-done(((f32[2048,512]{0,1:T(8,128)}), f32[2048,256]{0,1:T(8,128)}) %reduce-scatter.2.cloned.1.call-update) | async-done | bytes 2097168 | tf_op jit(solution)/shard_map/reduce_scatter | solution.py:23
  298.4 0.0 copy-done.2
  298.4 0.0 copy-done.3
  298.4 0.0 copy-start
  298.4 2.1 fusion.8
  300.5 33.2 %pmax.7 = f32[256]{0:T(256)S(1)} all-reduce(f32[256]{0:T(256)S(1)} %fusion.8), channel_id=1, replica_groups=mesh['row'=16,'col'=2] {'row'}, use_global_device_ids=true, to_apply=%region_2.0 | all-reduce | flops 256 | bytes 2048 | tf_op jit(solution)/shard_map/pmax | solution.py:26
  333.7 0.0 copy-done
  333.7 0.6 fusion.7
  334.2 29.5 %psum.7 = f32[256]{0:T(256)S(1)} all-reduce(f32[256]{0:T(256)S(1)} %fusion.7), channel_id=1, replica_groups=mesh['row'=16,'col'=2] {'row'}, use_global_device_ids=true, to_apply=%region_4.0 | all-reduce | flops 256 | bytes 2048 | tf_op jit(solution)/shard_map/psum | solution.py:28
  363.7 0.0 copy-done.4
  363.7 0.6 log_subtract_fusion
  364.3 0.6 multiply_convert_fusion
  364.9 1.3 copy.9
Async XLA Ops:
  7.2 80.6 %all-gather.2.cloned.1.call-start = ((), (), s32[]{:S(2)}) async-start(), calls=%async_computation.2 | async-start | bytes 8912896 | tf_op jit(solution)/shard_map/all_gather | solution.py:11
  87.8 7.1 %copy-start.1 = (bf16[256,256]{1,0:T(8,128)(2,1)S(1)}, bf16[256,256]{1,0:T(8,128)(2,1)}, u32[]{:S(2)}) copy-start(bf16[256,256]{1,0:T(8,128)(2,1)} %param.8) | copy-start | bytes 393220
  87.8 102.8 %all-to-all-start = ((bf16[2,1,16384,128]{3,2,1,0:T(8,128)(2,1)}), bf16[2,1,16384,128]{3,2,1,0:T(8,128)(2,1)}, u32[]{:S(2)}, u32[]{:S(2)}) async-start(bf16[2,1,16384,128]{3,2,1,0:T(8,128)(2,1)} %bitcast.31), calls=%async_computation | async-start | bytes 16777216 | tf_op jit(solution)/shard_map/all_to_all | solution.py:14
  94.8 203.5 %reduce-scatter.2.cloned.1.call-start = ((), (), s32[]{:S(2)}) async-start(), calls=%async_computation.3 | async-start | bytes 6291456 | tf_op jit(solution)/shard_map/reduce_scatter | solution.py:23
  246.5 51.9 %copy-start.2 = (f32[2048]{0:T(1024)S(1)}, f32[2048]{0:T(1024)}, u32[]{:S(2)}) copy-start(f32[2048]{0:T(1024)} %param.9) | copy-start | bytes 24580
  246.5 51.9 %copy-start.3 = (f32[256]{0:T(256)S(1)}, f32[256]{0:T(256)}, u32[]{:S(2)}) copy-start(f32[256]{0:T(256)} %param.10) | copy-start | bytes 3076
  246.5 117.2 %copy-start.4 = (f32[256]{0:T(256)S(1)}, f32[256]{0:T(256)}, u32[]{:S(2)}) copy-start(f32[256]{0:T(256)} %param.11) | copy-start | bytes 3076
  298.4 35.3 %copy-start = (f32[2048,256]{0,1:T(8,128)S(1)}, f32[2048,256]{0,1:T(8,128)}, u32[]{:S(2)}) copy-start(f32[2048,256]{0,1:T(8,128)} %reduce-scatter.2.cloned.1.call-done) | copy-start | bytes 6291460
Sparse Core Ops, SparseCore 0:
  10.2 77.5 all-gather.1
  246.6 51.6 reduce-scatter.1
where the time goes:
time: 373 us
  blocking collectives  158 us (42%)
  waiting for transfers between devices  132 us (35%)
  matrix products  55.9 us (15%)
  between operations  14.1 us (4%)
  starting transfers between devices  7.13 us (2%)
  other arithmetic  3.86 us (1%)
    all_gather x1, blocking collectives, body(): second_full = lax.all_gather(dist_second, 'col', axis=1, tiled=True)  95.7 us
    all_gather x1, waiting for transfers between devices, body(): stacked = lax.all_gather(coupling, 'row', axis=0, tiled=True)  79.9 us
    reduce_scatter x1, waiting for transfers between devices, body(): lax.psum_scatter(partial_value, 'col', scatter_dimension=1, tiled=True)  51.8 us
    dot_general x1, matrix products, body(): jnp.dot(dist_first, product, preferred_element_type=jnp.float32)  44.3 us
    pmax x1, blocking collectives, body(): highest = lax.pmax(local_high, 'row')  33.2 us
    psum x1, blocking collectives, body(): column_sum = lax.psum(jnp.sum(weights, axis=0), 'row')  29.5 us
    dot_general x1, matrix products, body(): jnp.einsum('jnk,jkq->nq', traded[0], second_blocks, preferred_element_typ...  11.6 us
  transfers between devices with their start and end apart: 3, of which 2 were waited for; matrix products, arithmetic and copies ran while one was open for 0% of the time, Pallas kernels for 0%

commit v1 on v0

v1 whole, which is shorter than its diff:
```python
import functools

import jax
import jax.numpy as jnp
from jax import lax
from jax.experimental import pallas as pl
from jax.experimental.pallas import tpu as pltpu
from jax.sharding import PartitionSpec as P

LEVELS = 4
SUBS = 4
CHUNKS = 8
SEND = jnp.float32
MESH = pl.DeviceIdType.MESH


def kernel(
    n_rows, width, total,
    dist_ref, coup_ref, second_ref, rowpot_ref, cost_ref, mass_ref,
    trans_ref, pot_ref,
    call, sfull, dbuf, pbuf, acc, rpb, exs, exr, stat, cmax,
    d_sem, loc_sem, y_send, z_send, x_send, c_send, recv,
    s_send, s_recv, e_send, e_recv, st_send, st_recv,
):
    m = coup_ref.shape[0]
    mp = m // SUBS
    mc = m // CHUNKS
    nb = n_rows // (2 * LEVELS)
    half = second_ref.shape[1]
    kc = coup_ref.shape[1]
    n_sub = 2 * nb
    steps = 2 * SUBS

    r = lax.axis_index("row")
    y = lax.axis_index("col")
    core = lax.rem(r, 2)
    q = lax.div(r, 2)
    b = lax.rem(q, nb)
    a = lax.div(q, nb)

    def flip(v, col):
        return v + col * (LEVELS - 1 - 2 * v)

    at = flip(a, y)

    def row_of(level, bb, kk):
        return (flip(level, y) * nb + bb) * 2 + kk

    def slot(level, bb, kk, col):
        return ((level + col * (1 - 2 * level)) * nb + bb) * 2 + kk

    def region(level, bb, kk, kind, p, col):
        start = pl.multiple_of(slot(level, bb, kk, col) * m + p * mp, mp)
        return call.at[pl.ds(start, mp), pl.ds(pl.multiple_of(kind * kc, kc), kc)]

    partner = (r, 1 - y)
    first = jnp.where(at == 0, 0, 1)

    def order(j):
        late = lax.div(j, SUBS)
        level = first + late * (1 - 2 * first)
        return level, j - late * SUBS

    def fetch(j, start):
        level, p = order(j)
        buf = lax.rem(j, 2)
        for i in range(n_sub):
            col0 = pl.multiple_of(slot(level, i // 2, i % 2, y) * m + p * mp, mp)
            cp = pltpu.make_async_copy(
                dist_ref.at[:, pl.ds(col0, mp)],
                dbuf.at[buf, :, pl.ds(i * mp, mp)],
                d_sem.at[buf, i],
            )
            if start:
                cp.start()
            else:
                cp.wait()

    fetch(0, True)

    barrier = pltpu.get_barrier_semaphore()

    @pl.loop(1, n_rows)
    def _(j):
        pl.semaphore_signal(
            barrier, inc=1, device_id=(lax.rem(r + j, n_rows), y), device_id_type=MESH
        )

    pl.semaphore_signal(barrier, inc=1, device_id=partner, device_id_type=MESH)
    pl.semaphore_wait(barrier, n_rows)

    second_copy = pltpu.make_async_remote_copy(
        src_ref=second_ref, dst_ref=sfull.at[:, pl.ds(half, half)],
        send_sem=s_send, recv_sem=s_recv, device_id=partner, device_id_type=MESH,
    )
    second_copy.start()
    second_local = pltpu.make_async_copy(
        second_ref, sfull.at[:, pl.ds(0, half)], loc_sem.at[0]
    )
    second_local.start()

    def y_copy(p):
        return pltpu.make_async_remote_copy(
            src_ref=coup_ref.at[pl.ds(p * mp, mp), :],
            dst_ref=region(LEVELS - 1 - at, b, core, y, p, 1 - y),
            send_sem=y_send.at[p],
            recv_sem=recv.at[LEVELS - 1 - at, b, core, y, p],
            device_id=partner, device_id_type=MESH,
        )

    @pl.when(at >= 2)
    def _():
        for p in range(SUBS):
            y_copy(p).start()

    def own_copy():
        start = pl.multiple_of(slot(at, b, core, y) * m, m)
        return pltpu.make_async_copy(
            coup_ref,
            call.at[pl.ds(start, m), pl.ds(pl.multiple_of(y * kc, kc), kc)],
            loc_sem.at[1],
        )

    @pl.when(at < 2)
    def _():
        own_copy().start()
        own_copy().wait()

    second_local.wait()

    def copy(level, bb, kk, kind, p, send_sem, device):
        ref = region(level, bb, kk, kind, p, y)
        return pltpu.make_async_remote_copy(
            src_ref=ref, dst_ref=ref, send_sem=send_sem,
            recv_sem=recv.at[level, bb, kk, kind, p],
            device_id=device, device_id_type=MESH,
        )

    def up_copy(level, kind, p):
        dev = (row_of(jnp.minimum(at + 1, LEVELS - 1), b, core), y)
        return copy(level, b, core, kind, p, z_send.at[0, level, kind, p], dev)

    def down_copy(level, kind, p):
        dev = (row_of(jnp.maximum(at - 1, 0), b, core), y)
        return copy(level, b, core, kind, p, z_send.at[1, level, kind, p], dev)

    def side_copy(j, level, kind, p):
        dev = (row_of(at, lax.rem(b + j, nb), core), y)
        return copy(level, b, core, kind, p, x_send.at[j, level, kind, p], dev)

    def core_copy(bb, level, kind, p):
        dev = (row_of(at, b, 1 - core), y)
        return copy(level, bb, core, kind, p, c_send.at[bb, level, kind, p], dev)

    def wait_piece(level, bb, kk, kind, p):
        dev = (row_of(at, b, 1 - core), y)
        copy(level, bb, kk, kind, p, c_send.at[bb, level, kind, p], dev).wait_recv()

    def sends_up(level):
        return jnp.logical_or(
            jnp.logical_and(at == 0, level == 0), jnp.logical_or(at == 1, at == 2)
        )

    def sends_down(level):
        return jnp.logical_and(at == 1, level == 1)

    def forward(level, p):
        for late in range(2):
            kind = y + late * (1 - 2 * y)
            if late == 0:
                @pl.when(level != at)
                def _():
                    wait_piece(level, b, core, kind, p)
            else:
                wait_piece(level, b, core, kind, p)

            @pl.when(sends_up(level))
            def _():
                up_copy(level, kind, p).start()

            @pl.when(sends_down(level))
            def _():
                down_copy(level, kind, p).start()

            for j in range(1, nb):
                side_copy(j, level, kind, p).start()
            core_copy(b, level, kind, p).start()

    def cross(level, p):
        for j in range(1, nb):
            bb = lax.rem(b + j, nb)
            for kind in range(2):
                wait_piece(level, bb, core, kind, p)
                core_copy(bb, level, kind, p).start()

    def gathered(level, p):
        for j in range(nb):
            bb = lax.rem(b + j, nb)
            for kind in range(2):
                wait_piece(level, bb, 1 - core, kind, p)

    def make_product(level, p):
        for i in range(n_sub):
            start = pl.multiple_of(slot(level, i // 2, i % 2, y) * m + p * mp, mp)
            pbuf[i * mp:(i + 1) * mp, :] = jnp.dot(
                call[pl.ds(start, mp), :], sfull[...], preferred_element_type=jnp.float32
            ).astype(jnp.bfloat16)

    forward(*order(0))

    for i in range(m // 128):
        line = jnp.broadcast_to(rowpot_ref[i:i + 1, :], (128, 128))
        rpb[i * 128:(i + 1) * 128, :] = line.T

    second_copy.wait_recv()

    def ex_copy(c):
        rows = pl.ds(pl.multiple_of(c * mc, mc), mc)
        return pltpu.make_async_remote_copy(
            src_ref=exs.at[rows, :], dst_ref=exr.at[rows, :],
            send_sem=e_send.at[c], recv_sem=e_recv.at[c],
            device_id=partner, device_id_type=MESH,
        )

    @pl.loop(0, steps)
    def _(j):
        level, p = order(j)

        @pl.when(j + 1 < steps)
        def _():
            forward(*order(j + 1))
            fetch(j + 1, True)

        cross(level, p)
        gathered(level, p)
        make_product(level, p)
        fetch(j, False)
        buf = lax.rem(j, 2)

        @pl.loop(0, CHUNKS)
        def _(c):
            rows = pl.ds(pl.multiple_of(c * mc, mc), mc)
            value = jnp.dot(
                dbuf[buf, rows, :], pbuf[...], preferred_element_type=jnp.float32
            )

            @pl.when(j == 0)
            def _():
                acc[rows, :] = value

            @pl.when(jnp.logical_and(j > 0, j < steps - 1))
            def _():
                acc[rows, :] += value

            @pl.when(j == steps - 1)
            def _():
                done = acc[rows, :] + value
                acc[rows, 0:half] = done[:, 0:half]
                exs[rows, :] = done[:, half:].astype(SEND)
                ex_copy(c).start()

    @pl.loop(0, CHUNKS)
    def _(c):
        ex_copy(c).wait()
        rows = pl.ds(pl.multiple_of(c * mc, mc), mc)
        gradient = acc[rows, 0:half] + exr[rows, :].astype(jnp.float32)
        pot = jnp.concatenate([rpb[rows, :]] * (half // 128), axis=1)
        scores = pot + 2.0 * gradient - cost_ref[...]
        high = jnp.max(scores, axis=0, keepdims=True)
        weights = jnp.exp(scores - high)
        acc[rows, 0:half] = weights
        cmax[c, 0:1, :] = high
        cmax[c, 1:2, :] = jnp.sum(weights, axis=0, keepdims=True)

    highs = cmax[:, 0, :]
    high = jnp.max(highs, axis=0, keepdims=True)
    sums = jnp.sum(cmax[:, 1, :] * jnp.exp(highs - high), axis=0, keepdims=True)
    stat[r, 0:1, :] = high
    stat[r, 1:2, :] = sums

    def stat_copy(j, src):
        return pltpu.make_async_remote_copy(
            src_ref=stat.at[src], dst_ref=stat.at[src],
            send_sem=st_send.at[j], recv_sem=st_recv.at[src],
            device_id=(lax.rem(r + j, n_rows), y), device_id_type=MESH,
        )

    @pl.loop(1, n_rows)
    def _(j):
        stat_copy(j, r).start()

    second_copy.wait_send()

    @pl.when(at >= 2)
    def _():
        for p in range(SUBS):
            y_copy(p).wait_send()

    @pl.loop(0, steps)
    def _(j):
        level, p = order(j)
        for kind in range(2):
            @pl.when(sends_up(level))
            def _():
                up_copy(level, kind, p).wait_send()

            @pl.when(sends_down(level))
            def _():
                down_copy(level, kind, p).wait_send()

            for i in range(1, nb):
                side_copy(i, level, kind, p).wait_send()
            for bb in range(nb):
                core_copy(bb, level, kind, p).wait_send()

    @pl.loop(1, n_rows)
    def _(j):
        stat_copy(j, lax.rem(r + j, n_rows)).wait_recv()

    all_high = stat[:, 0, :]
    all_sum = stat[:, 1, :]
    highest = jnp.max(all_high, axis=0, keepdims=True)
    column_sum = jnp.sum(all_sum * jnp.exp(all_high - highest), axis=0, keepdims=True)
    pot_ref[...] = jnp.log(mass_ref[...]) - highest - jnp.log(column_sum)
    scale = total * mass_ref[...] / column_sum

    @pl.loop(0, CHUNKS)
    def _(c):
        rows = pl.ds(pl.multiple_of(c * mc, mc), mc)
        factor = jnp.exp(cmax[c, 0:1, :] - highest) * scale
        trans_ref[rows, :] = (acc[rows, 0:half] * factor).astype(trans_ref.dtype)

    @pl.loop(1, n_rows)
    def _(j):
        stat_copy(j, r).wait_send()


def body(n_rows, total, dist_first, coupling, dist_second, row_potential, column_cost, column_mass):
    m, width = dist_first.shape
    kc = coupling.shape[1]
    depth, half = dist_second.shape
    nb = n_rows // (2 * LEVELS)
    block = width // (2 * SUBS)
    vmem = pl.BlockSpec(memory_space=pltpu.VMEM)
    hbm = pl.BlockSpec(memory_space=pl.ANY)
    dma = pltpu.SemaphoreType.DMA
    transport, potential = pl.pallas_call(
        functools.partial(kernel, n_rows, width, float(total)),
        out_shape=(
            jax.ShapeDtypeStruct((m, half), jnp.bfloat16),
            jax.ShapeDtypeStruct((1, half), jnp.float32),
        ),
        in_specs=[hbm, vmem, vmem, vmem, vmem, vmem],
        out_specs=(vmem, vmem),
        scratch_shapes=[
            pltpu.VMEM((width, depth), jnp.bfloat16),
            pltpu.VMEM((depth, 2 * half), jnp.bfloat16),
            pltpu.VMEM((2, m, block), jnp.bfloat16),
            pltpu.VMEM((block, 2 * half), jnp.bfloat16),
            pltpu.VMEM((m, 2 * half), jnp.float32),
            pltpu.VMEM((m, 128), jnp.float32),
            pltpu.VMEM((m, half), SEND),
            pltpu.VMEM((m, half), SEND),
            pltpu.VMEM((n_rows, 8, half), jnp.float32),
            pltpu.VMEM((CHUNKS, 8, half), jnp.float32),
            dma((2, 2 * nb)),
            dma((2,)),
            dma((SUBS,)),
            dma((2, 2, 2, SUBS)),
            dma((nb, 2, 2, SUBS)),
            dma((nb, 2, 2, SUBS)),
            dma((2, nb, 2, 2, SUBS)),
            dma, dma,
            dma((CHUNKS,)), dma((CHUNKS,)),
            dma((n_rows,)), dma((n_rows,)),
        ],
        compiler_params=pltpu.CompilerParams(
            collective_id=0, has_side_effects=True, vmem_limit_bytes=60 * 1024 * 1024
        ),
        cost_estimate=pl.CostEstimate(
            flops=2 * m * width * 2 * half + 2 * width * depth * 2 * half,
            bytes_accessed=m * width * 2, transcendentals=m * half,
        ),
    )(
        dist_first, coupling, dist_second,
        row_potential.reshape(m // 128, 128),
        column_cost.reshape(1, half), column_mass.reshape(1, half),
    )
    return transport, potential.reshape(half)


def solution(mesh):
    n_rows = mesh.shape["row"]

    def run(dist_first, *rest):
        in_specs = (P("row", "col"), P("row", "col"), P(None, "col"), P("row"), P("col"), P("col"))
        out_specs = (P("row", "col"), P("col"))
        return jax.shard_map(
            functools.partial(body, n_rows, dist_first.shape[0]),
            mesh=mesh, in_specs=in_specs, out_specs=out_specs, check_vma=False,
        )(dist_first, *rest)

    return run
```

time: 373 us -> 154 us (0.41)
  blocking collectives: 158 us -> 0 us
  Pallas kernels: 0 us -> 150 us
  waiting for transfers between devices: 132 us -> 0 us
  matrix products: 55.9 us -> 0 us
  between operations: 14.1 us -> 0.64 us
  starting transfers between devices: 7.13 us -> 0 us
  other arithmetic: 3.86 us -> 0 us
    pallas_call x0 -> x1, Pallas kernels: none -> 150 us  [body(): pl.pallas_call(functools.partial(kernel, n_rows, width, float(total)), ou...]
    all_gather x1 -> x0, blocking collectives: 95.7 us -> none  [body(): second_full = lax.all_gather(dist_second, 'col', axis=1, tiled=True)]
    all_gather x1 -> x0, waiting for transfers between devices: 79.9 us -> none  [body(): stacked = lax.all_gather(coupling, 'row', axis=0, tiled=True)]
    dot_general x2 -> x0, matrix products: 55.9 us -> none  [the longest x1 44.3 us: body(): jnp.dot(dist_first, product, preferred_element_type=jnp.float32)]
    reduce_scatter x1 -> x0, waiting for transfers between devices: 51.8 us -> none  [body(): lax.psum_scatter(partial_value, 'col', scatter_dimension=1, tiled=True)]
    pmax x1 -> x0, blocking collectives: 33.2 us -> none  [body(): highest = lax.pmax(local_high, 'row')]
    psum x1 -> x0, blocking collectives: 29.5 us -> none  [body(): column_sum = lax.psum(jnp.sum(weights, axis=0), 'row')]
    all_to_all x1 -> x0, starting transfers between devices: 7.05 us -> none  [body(): lax.all_to_all(stacked, 'col', split_axis=0, concat_axis=1, tiled=True)]
  transfers between devices with their start and end apart: 3 -> 0, of which waited for: 2 -> 0; matrix products, arithmetic and copies ran while one was open for 0% -> 0% of each run, Pallas kernels for 0% -> 0%
where the time goes in v1:
time: 154 us
  Pallas kernels  150 us (97%)
  local copies, waits for them, and re-layouts  3.5 us (2%)
    pallas_call x1, Pallas kernels, body(): pl.pallas_call(functools.partial(kernel, n_rows, width, float(total)), ou...  150 us
    unnamed x2, local copies, waits for them, and re-layouts  3.5 us

profile of v1, /device:TPU:0, one launch (start us, length us, event | category | flops | bytes accessed | tf_op | source)
XLA Modules:
  0.0 154.0 jit_solution(6187289601682710042)
XLA Ops:
  0.6 149.8 %shard_map.77 = (bf16[2048,256]{1,0:T(8,128)(2,1)}, f32[1,256]{1,0:T(1,128)}) custom-call(bf16[2048,16384]{1,0:T(8,128)(2,1)} %dist_ref.1, bf16[2048,128]{1,0:T(8,128)(2,1)} %coup_ref.1, bf16[256,256]{1,0:T(8,128)(2,1)} %second_ref.1, f32[16,128]{1,0:T(8,128)} %bitcast.5, f32[1,256]{1,0:T(1,128)} %bitcast.6, f32[1,256]{1,0:T(1,128)} %bitcast.7), custom_call_target="tpu_custom_call" | custom-call | flops 38654705664 | bytes 67108864 | tf_op jit(solution)/shard_map/pallas_call | solution.py:347
  150.5 2.3 %copy.10 = bf16[2048,256]{1,0:T(8,128)(2,1)} copy(bf16[2048,256]{1,0:T(8,128)(2,1)} %get-tuple-element.8) | data formatting | bytes 2097152
  152.7 1.2 copy.11
